TPU v7x, 128 devices: a whole 4x4x4 slice. The times are simulated.
128 devices in a mesh: dp: 2 (over core), vocab: 64 (over z, y, x).
Axes of the slice: x: 4, y: 4, z: 4, core: 2. Of those that a mesh axis runs over, the one named last changes fastest.
Arguments:
- hidden: bfloat16 [384, 8192], P('dp', 'vocab'), may hold values from -12 to 12
- tangent_hidden: bfloat16 [384, 8192], P('dp', 'vocab'), may hold values from -6 to 6
- head: bfloat16 [8192, 65536], P('dp', 'vocab'), may hold values from -1 to 1
- tangent_head: bfloat16 [8192, 65536], P('dp', 'vocab'), may hold values from -0.0625 to 0.0625
- allowed: int32 [384, 512], P('dp', 'vocab'), may hold values from 0 to 1, as said below
Outputs:
- head_product: bfloat16 [8192, 65536], P('dp', 'vocab')
- hidden_product: bfloat16 [384, 8192], P('dp', 'vocab')
Inputs may be any that keep to these rules, and one draw needn't show every extreme that they name: Every token allows block 0. The chance that a block is allowed rises along the vocabulary from about a tenth to about nine tenths.
All inputs are finite; a program needn't handle non-finite values.
Results may differ from a plain program's by a relative error of at most 0.012.
Values may be sent and summed in bfloat16 or wider, within the bound.
No kernel may reach another device: no remote copies, remote signals or barrier semaphores. Data moves between devices by JAX's collectives and lax.ppermute only.
A program may use at most 192 MiB of HBM per device.

v0:
```python
import jax
import jax.numpy as jnp
from jax import lax
from jax.sharding import PartitionSpec as P


def contract_rows(left, right):
    return lax.dot_general(
        left, right, (((0,), (0,)), ((), ())), preferred_element_type=jnp.float32
    )


def contract_cols(left, right):
    return lax.dot_general(
        left, right, (((1,), (1,)), ((), ())), preferred_element_type=jnp.float32
    )


def shards(hidden, tangent_hidden, head, tangent_head, allowed):
    tok_rows = hidden.shape[0]
    voc_cols = head.shape[1]
    groups = lax.axis_size("dp")
    rows_full, trows_full = (
        lax.all_gather(hidden, "vocab", axis=1, tiled=True),
        lax.all_gather(tangent_hidden, "vocab", axis=1, tiled=True),
    )
    rows_part, trows_part = (
        lax.all_to_all(rows_full, "dp", split_axis=1, concat_axis=0, tiled=True),
        lax.all_to_all(trows_full, "dp", split_axis=1, concat_axis=0, tiled=True),
    )
    logit_part = jnp.dot(rows_part, head, preferred_element_type=jnp.float32)
    tangent_part = jnp.dot(trows_part, head, preferred_element_type=jnp.float32) + jnp.dot(
        rows_part, tangent_head, preferred_element_type=jnp.float32
    )
    logits, tangent = (
        lax.psum_scatter(logit_part, "dp", scatter_dimension=0, tiled=True),
        lax.psum_scatter(tangent_part, "dp", scatter_dimension=0, tiled=True),
    )
    allowed_cols = jnp.broadcast_to(
        (allowed > 0)[:, :, None], (tok_rows, voc_cols // 128, 128)
    ).reshape(tok_rows, voc_cols)
    local_top = jnp.max(jnp.where(allowed_cols, logits, -jnp.inf), axis=1)
    top_logit = lax.pmax(local_top, "vocab")
    weights = jnp.exp(jnp.where(allowed_cols, logits - top_logit[:, None], -jnp.inf))
    denominator, moment = lax.psum(
        (jnp.sum(weights, axis=1), jnp.sum(weights * tangent, axis=1)), "vocab"
    )
    probs = weights / denominator[:, None]
    expected = moment / denominator
    product = (probs * (tangent - expected[:, None])).astype(jnp.bfloat16)
    product_all = lax.all_gather(product, "dp", axis=0, tiled=True)
    summed_head = jnp.zeros((head.shape[0], voc_cols), jnp.float32)
    for group in range(groups):
        rows_group = rows_part[group * tok_rows : (group + 1) * tok_rows]
        product_group = product_all[group * tok_rows : (group + 1) * tok_rows]
        summed_head = summed_head + contract_rows(rows_group, product_group).astype(
            jnp.bfloat16
        ).astype(jnp.float32)
    head_product = summed_head.astype(jnp.bfloat16)
    partial_term = contract_cols(product_all, head)
    regrouped = lax.all_to_all(
        partial_term.astype(jnp.bfloat16), "dp", split_axis=0, concat_axis=1, tiled=True
    ).astype(partial_term.dtype)
    hidden_product = lax.psum_scatter(regrouped, "vocab", scatter_dimension=1, tiled=True).astype(
        jnp.bfloat16
    )
    return (head_product, hidden_product)


def solution(mesh):
    placed = (
        P("dp", "vocab"),
        P("dp", "vocab"),
        P("dp", "vocab"),
        P("dp", "vocab"),
        P("dp", "vocab"),
    )
    return jax.shard_map(
        shards,
        mesh=mesh,
        in_specs=placed,
        out_specs=(P("dp", "vocab"), P("dp", "vocab")),
        check_vma=False,
    )
```

profile of v0, /device:TPU:1, one launch (start us, length us, event | category | flops | bytes accessed | tf_op | source)
XLA Modules:
  0.0 780.3 jit_solution(16046998692385807610)
XLA Ops:
  7.2 0.0 all-gather.3.cloned.1.call-start
  7.2 0.7 all-gather.3.cloned.1.call-update
  7.9 0.0 all-gather.5.cloned.1.call-start
  7.9 0.7 all-gather.5.cloned.1.call-update
  8.6 0.0 reduce-scatter.4.cloned.1.call-start
  8.7 76.6 %all-gather.3.cloned.1.call-done = bf16[192,8192]{1,0:T(8,128)(2,1)} async-done(((bf16[192,128]{1,0:T(8,128)(2,1)}), bf16[192,8192]{1,0:T(8,128)(2,1)}) %all-gather.3.cloned.1.call-update) | async-done | bytes 3145744 | tf_op jit(solution)/shard_map/all_gather | solution.py:24
  85.3 0.0 copy-start.3
  85.3 2.4 copy.38
  87.6 7.7 all_to_all.51
  95.3 0.0 copy-done.3
  95.3 4.5 fusion.5
  99.9 0.0 reduce-scatter.4.cloned.1.call-update
  99.9 0.0 reduce-scatter.6.cloned.1.call-start
  100.0 59.5 %all-gather.5.cloned.1.call-done = bf16[192,8192]{1,0:T(8,128)(2,1)} async-done(((bf16[192,128]{1,0:T(8,128)(2,1)}), bf16[192,8192]{1,0:T(8,128)(2,1)}) %all-gather.5.cloned.1.call-update) | async-done | bytes 3145744 | tf_op jit(solution)/shard_map/all_gather | solution.py:25
  159.4 2.2 copy.37
  161.7 0.0 slice-start
  161.7 7.7 all_to_all.52
  169.4 0.0 slice-start.1
  169.4 6.5 fusion.6
  175.8 0.0 slice-done
  175.8 0.0 slice-done.1
  175.9 0.0 copy-start.2
  175.9 4.6 convolution_add_fusion
  180.4 0.0 reduce-scatter.6.cloned.1.call-update
  180.5 0.0 reduce-scatter.8.cloned.1.call-start
  180.5 0.0 copy-done.2
  180.5 0.1 copy.18
  180.7 0.0 reduce-scatter.4.cloned.1.call-done
  180.7 0.3 broadcast_in_dim.7
  181.0 1.3 select_reduce_fusion
  182.3 148.2 %pmax.7 = f32[192]{0:T(256)S(1)} all-reduce(f32[192]{0:T(256)S(1)} %select_reduce_fusion), channel_id=1, replica_groups=mesh['dp'=2,'vocab'=64] {'vocab'}, use_global_device_ids=true, to_apply=%region_2.3 | all-reduce | flops 192 | bytes 1536 | tf_op jit(solution)/shard_map/pmax | solution.py:43
  330.5 1.8 fusion.4
  332.3 144.2 %all-reduce = (f32[192]{0:T(256)S(1)}, f32[192]{0:T(256)S(1)}) all-reduce(f32[192]{0:T(256)S(1)} %get-tuple-element.11, f32[192]{0:T(256)S(1)} %get-tuple-element.10), channel_id=1, replica_groups=mesh['dp'=2,'vocab'=64] {'vocab'}, use_global_device_ids=true, to_apply=%region_7.8 | all-reduce | flops 384 | bytes 3072 | tf_op jit(solution)/shard_map/psum | solution.py:45
  476.5 1.7 multiply_convert_fusion
  478.2 57.8 %all_gather.11 = bf16[384,1024]{1,0:T(8,128)(2,1)S(1)} all-gather(bf16[192,1024]{1,0:T(8,128)(2,1)S(1)} %multiply_convert_fusion), channel_id=1, replica_groups=mesh['dp'=2,'vocab'=64] {'dp'}, dimensions={0}, use_global_device_ids=true | all-gather | bytes 1179648 | tf_op jit(solution)/shard_map/all_gather | solution.py:51
  536.0 9.5 %convolution_convert_fusion = bf16[384,4096]{1,0:T(8,128)(2,1)S(1)} fusion(bf16[384,1024]{1,0:T(8,128)(2,1)S(1)} %all_gather.11, bf16[4096,1024]{1,0:T(8,128)(2,1)} %param.7), kind=kOutput, calls=%fused_computation.3 | convolution fusion | flops 3222798336 | bytes 12320768 | tf_op jit(solution)/shard_map/dot_general | solution.py:14
  545.4 0.0 copy-done
  545.4 6.3 all_to_all.53
  551.8 0.8 convert_bitcast_fusion
  552.5 3.1 copy.25
  555.6 0.0 reduce-scatter.8.cloned.1.call-update
  555.7 0.0 copy-start.1
  555.7 3.4 fusion.1
  559.1 0.0 copy-done.1
  559.1 5.7 fusion
  564.8 12.0 %copy.22 = bf16[4096,1024]{1,0:T(8,128)(2,1)} copy(bf16[4096,1024]{0,1:T(8,128)(2,1)} %fusion) | data formatting | bytes 16777216
  576.8 195.5 %reduce-scatter.8.cloned.1.call-done = f32[192,128]{1,0:T(8,128)} async-done(((f32[192,8192]{1,0:T(8,128)}), f32[192,128]{1,0:T(8,128)}) %reduce-scatter.8.cloned.1.call-update) | async-done | bytes 98320 | tf_op jit(solution)/shard_map/reduce_scatter | solution.py:64
  772.2 1.5 convert_element_type.51
  (5 shorter events, 0.0 us)
Async XLA Ops:
  7.2 78.1 %all-gather.3.cloned.1.call-start = ((), (), s32[]{:S(2)}) async-start(), calls=%async_computation.6 | async-start | bytes 3194880 | tf_op jit(solution)/shard_map/all_gather | solution.py:24
  7.9 151.5 %all-gather.5.cloned.1.call-start = ((), (), s32[]{:S(2)}) async-start(), calls=%async_computation.8 | async-start | bytes 3194880 | tf_op jit(solution)/shard_map/all_gather | solution.py:25
  8.6 172.0 %reduce-scatter.4.cloned.1.call-start = ((), (), s32[]{:S(2)}) async-start(), calls=%async_computation.7 | async-start | bytes 2359296 | tf_op jit(solution)/shard_map/reduce_scatter | solution.py:36
  85.3 10.1 %copy-start.3 = (bf16[4096,1024]{1,0:T(8,128)(2,1)S(1)}, bf16[4096,1024]{1,0:T(8,128)(2,1)}, u32[]{:S(2)}) copy-start(bf16[4096,1024]{1,0:T(8,128)(2,1)} %param.7) | copy-start | bytes 25165828
  99.9 230.6 %reduce-scatter.6.cloned.1.call-start = ((), (), s32[]{:S(2)}) async-start(), calls=%async_computation.9 | async-start | bytes 2359296 | tf_op jit(solution)/shard_map/reduce_scatter | solution.py:37
  161.7 14.2 %slice-start = ((s8[8388608]{0:T(1024)(128)(4,1)}), s8[4194304]{0:T(1024)(128)(4,1)S(1)}, s32[]{:S(2)}) async-start(s8[8388608]{0:T(1024)(128)(4,1)} %bitcast.59), calls=%async_computation.11 | async-start | bytes 8388608
  169.4 6.5 slice-start.1
  175.9 4.6 copy-start.2
  180.5 591.8 %reduce-scatter.8.cloned.1.call-start = ((), (), s32[]{:S(2)}) async-start(), calls=%async_computation.10 | async-start | bytes 6389760 | tf_op jit(solution)/shard_map/reduce_scatter | solution.py:64
  536.0 9.5 %copy-start = (bf16[384,1024]{1,0:T(8,128)(2,1)}, bf16[384,1024]{1,0:T(8,128)(2,1)S(1)}, u32[]{:S(2)}) copy-start(bf16[384,1024]{1,0:T(8,128)(2,1)S(1)} %all_gather.11) | copy-start | bytes 2359300
  555.7 3.5 copy-start.1
Sparse Core Ops, SparseCore 0:
  10.7 74.5 all-gather.2
  87.9 71.4 all-gather.4
  161.8 12.2 reduce-scatter.3
  180.6 10.5 reduce-scatter.5
  555.8 216.4 reduce-scatter.7
where the time goes:
time: 782 us; the launch traced here: 780 us
  blocking collectives  372 us (48%)
  waiting for transfers between devices  333 us (43%)
  matrix products  34.1 us (4%)
  local copies, waits for them, and re-layouts  20.1 us (3%)
  between operations  13.9 us (2%)
    reduce_scatter x1, waiting for transfers between devices, shards(): lax.psum_scatter(regrouped, 'vocab', scatter_dimension=1, tiled=True)  195 us
    pmax x1, blocking collectives, shards(): top_logit = lax.pmax(local_top, 'vocab')  148 us
    psum x1, blocking collectives, shards(): lax.psum((jnp.sum(weights, axis=1), jnp.sum(weights * tangent, axis=1)),...  144 us
    all_gather x1, waiting for transfers between devices, shards(): lax.all_gather(hidden, 'vocab', axis=1, tiled=True)  76.6 us
    all_gather x1, waiting for transfers between devices, shards(): lax.all_gather(tangent_hidden, 'vocab', axis=1, tiled=True)  59.5 us
    all_gather x1, blocking collectives, shards(): product_all = lax.all_gather(product, 'dp', axis=0, tiled=True)  57.8 us
  transfers between devices with their start and end apart: 5, of which 3 were waited for; matrix products, arithmetic and copies ran while one was open for 6% of the time, Pallas kernels for 0%

commit v1 on v0

v1 whole, which is shorter than its diff:
```python
import functools

import jax
import jax.numpy as jnp
from jax import lax
from jax.experimental import pallas as pl
from jax.experimental.pallas import tpu as pltpu
from jax.sharding import PartitionSpec as P

AXES = ("dp", "vocab")
SIDE = 4
TOK = 192
COLS = 1024
NEG = -1e30
VMEM = 48 * 1024 * 1024
F32 = jnp.float32
BF16 = jnp.bfloat16


def flat(k, z, y, x):
    return k * 64 + (z % 4) * 16 + (y % 4) * 4 + x % 4


def sites():
    return [(k, z, y, x) for k in range(2) for z in range(4) for y in range(4) for x in range(4)]


def shift(own, d):
    pairs = []
    for k, z, y, x in sites():
        along_x = (k == 0) == own
        target = flat(k, z, y, x + d) if along_x else flat(k, z, y + d, x)
        pairs.append((flat(k, z, y, x), target))
    return pairs


def swap_pairs():
    return [(flat(k, z, y, x), flat(1 - k, z, y, x)) for k, z, y, x in sites()]


def depth_groups():
    return [[flat(k, r + 2 * k, y, x) for r in range(4)] for k in range(2) for y in range(4) for x in range(4)]


def middle_groups():
    return [[flat(0, z, m, x) for m in range(4)] for z in range(4) for x in range(4)] + [
        [flat(1, z, y, m) for m in range(4)] for z in range(4) for y in range(4)
    ]


def plane_groups():
    return [[flat(0, r, m, x) for m in range(4) for r in range(4)] for x in range(4)] + [
        [flat(1, r + 2, y, m) for m in range(4) for r in range(4)] for y in range(4)
    ]


def permute(value, pairs):
    return lax.ppermute(value, AXES, pairs)


def exchange(value, groups):
    return lax.all_to_all(value, AXES, split_axis=0, concat_axis=0, tiled=True, axis_index_groups=groups)


def spread(value, groups):
    size = len(groups[0])
    return exchange(jnp.broadcast_to(value[None], (size,) + value.shape), groups)


def score_kernel(tab, *refs, own):
    chunks, heads, theads = refs[:4], refs[4:8], refs[8:12]
    i = pl.program_id(0)
    if own:
        got, allowed, weights, tangent, stats, acc, left = refs[12:]
    else:
        acc, left = refs[12:]

    @pl.when(i == 0)
    def _():
        acc[...] = jnp.zeros_like(acc)

    for d in range(4):

        @pl.when(i // 2 == d)
        def _():
            for j in range(2):
                for q in range(2):
                    at = 128 * (2 * j + q)
                    left[:, at : at + 128] = chunks[d][j, q]

    for n in range(4):
        cols = slice(256 * n, 256 * n + 256)
        right = jnp.concatenate([h[:, cols] for h in heads], axis=0)
        turn = jnp.concatenate([h[:, cols] for h in theads], axis=0)
        both = jnp.dot(left[...], right, preferred_element_type=F32)
        more = jnp.dot(left[:TOK], turn, preferred_element_type=F32)
        acc[:TOK, cols] += both[:TOK]
        acc[TOK:, cols] += both[TOK:] + more

    if own:

        @pl.when(i == 7)
        def _():
            lane = lax.broadcasted_iota(jnp.int32, (32, 128), 1)
            parts = []
            for r in range(0, TOK, 32):
                rows, trows = slice(r, r + 32), slice(TOK + r, TOK + r + 32)
                logit = acc[rows, :] + got[rows, :]
                tang = acc[trows, :] + got[trows, :]
                ok = jnp.concatenate(
                    [jnp.broadcast_to(allowed[rows, b : b + 1], (32, 128)) for b in range(8)], axis=1
                ) > 0
                logit = jnp.where(ok, logit, NEG)
                top = jnp.max(logit, axis=1, keepdims=True)
                w = jnp.where(ok, jnp.exp(logit - top), 0.0)
                den = jnp.sum(w, axis=1, keepdims=True)
                mom = jnp.sum(w * tang, axis=1, keepdims=True)
                weights[rows, :] = w
                tangent[rows, :] = tang
                parts.append(jnp.where(lane == 0, top, jnp.where(lane == 1, den, jnp.where(lane == 2, mom, 0.0))))
            first = jnp.concatenate(parts[:4], axis=0)
            second = jnp.concatenate(parts[4:] + [jnp.zeros((64, 128), F32)], axis=0)
            stats[0:4, :] = jnp.transpose(first)[0:4, :]
            stats[4:8, :] = jnp.transpose(second)[0:4, :]


def row_block(j, q):
    return pl.BlockSpec((128, COLS), lambda i, tab: (q * 16 + tab[2 * i + j], 0))


def whole(shape):
    return pl.BlockSpec(shape, lambda i, tab: (0,) * len(shape))


def chunk_block(d, rows):
    return pl.BlockSpec((2, 2, rows, 128), lambda i, tab: (jnp.clip(i - 2 * d, 0, 1), 0, 0, 0))


def scores(tab, chunks, head, tangent_head, got=None, allowed=None):
    own = got is not None
    blocks = [row_block(j, q) for j in range(2) for q in range(2)]
    in_specs = [chunk_block(d, 2 * TOK) for d in range(4)] + blocks + blocks
    operands = list(chunks) + [head] * 4 + [tangent_head] * 4
    scratch = [pltpu.VMEM((2 * TOK, 512), BF16)]
    if own:
        in_specs += [whole((2 * TOK, COLS)), whole((TOK, 8))]
        operands += [got, allowed]
        shapes = [(TOK, COLS), (TOK, COLS), (8, 128)]
        scratch = [pltpu.VMEM((2 * TOK, COLS), F32)] + scratch
    else:
        shapes = [(2 * TOK, COLS)]
    out = pl.pallas_call(
        functools.partial(score_kernel, own=own),
        grid_spec=pltpu.PrefetchScalarGridSpec(
            num_scalar_prefetch=1,
            grid=(8,),
            in_specs=in_specs,
            out_specs=[whole(s) for s in shapes],
            scratch_shapes=scratch,
        ),
        out_shape=[jax.ShapeDtypeStruct(s, F32) for s in shapes],
        compiler_params=pltpu.CompilerParams(vmem_limit_bytes=VMEM, dimension_semantics=("arbitrary",)),
        cost_estimate=pl.CostEstimate(flops=6 * TOK * 4096 * COLS, bytes_accessed=20 << 20, transcendentals=0),
        name="scores_own" if own else "scores_other",
    )(tab, *operands)
    return out if own else out[0]


def product_kernel(every, mine, weights, tangent, out):
    cols = []
    for g in range(2):
        top = every[:, 4 * g, :]
        best = jnp.max(top, axis=0, keepdims=True)
        scale = jnp.exp(top - best)
        den = jnp.sum(every[:, 4 * g + 1, :] * scale, axis=0, keepdims=True)
        mom = jnp.sum(every[:, 4 * g + 2, :] * scale, axis=0, keepdims=True)
        if g:
            real = lax.broadcasted_iota(jnp.int32, (1, 128), 1) < 64
            den = jnp.where(real, den, 1.0)
        factor = jnp.exp(mine[4 * g : 4 * g + 1, :] - best) / den
        mean = mom / den
        row = lax.broadcasted_iota(jnp.int32, (128, 128), 0)
        cols.append(jnp.transpose(jnp.where(row == 0, factor, jnp.where(row == 1, mean, 0.0))))
    both = jnp.concatenate([cols[0], cols[1][:64]], axis=0)
    for r in range(0, TOK, 32):
        rows = slice(r, r + 32)
        p = (weights[rows, :] * both[rows, 0:1]) * (tangent[rows, :] - both[rows, 1:2])
        out[rows, :] = p.astype(BF16)


def make_product(every, mine, weights, tangent):
    return pl.pallas_call(
        product_kernel,
        out_shape=jax.ShapeDtypeStruct((TOK, COLS), BF16),
        compiler_params=pltpu.CompilerParams(vmem_limit_bytes=VMEM),
        name="product",
    )(every, mine, weights, tangent)


def back_kernel(tab, product, *refs):
    heads, outs = refs[:4], refs[4:]
    i = pl.program_id(0)
    right = jnp.concatenate([h[...] for h in heads], axis=0)
    term = lax.dot_general(product[...], right, (((1,), (1,)), ((), ())), preferred_element_type=F32).astype(BF16)
    for d in range(4):

        @pl.when(i // 2 == d)
        def _():
            for j in range(2):
                for q in range(2):
                    at = 128 * (2 * j + q)
                    outs[d][j, q] = term[:, at : at + 128]


def back(tab, product, head):
    blocks = [row_block(j, q) for j in range(2) for q in range(2)]
    return pl.pallas_call(
        back_kernel,
        grid_spec=pltpu.PrefetchScalarGridSpec(
            num_scalar_prefetch=1,
            grid=(8,),
            in_specs=[whole((TOK, COLS))] + blocks,
            out_specs=[chunk_block(d, TOK) for d in range(4)],
        ),
        out_shape=[jax.ShapeDtypeStruct((4, 2, TOK, 128), BF16)] * 4,
        compiler_params=pltpu.CompilerParams(vmem_limit_bytes=VMEM, dimension_semantics=("arbitrary",)),
        cost_estimate=pl.CostEstimate(flops=2 * TOK * 4096 * COLS, bytes_accessed=10 << 20, transcendentals=0),
        name="hidden_back",
    )(tab, product, *([head] * 4))


def outer_kernel(tabs, *refs):
    mine, others, p_own, p_other, out, held = refs[:4], refs[4:8], refs[8], refs[9], refs[10], refs[11]
    i = pl.program_id(0)

    @pl.when(i == 0)
    def _():
        for d in range(4):
            for m in range(4):
                for q in range(2):
                    held[q * 16 + tabs[4 * d + m], 0:TOK, :] = mine[d][m, q]
                    held[q * 16 + tabs[16 + 4 * d + m], TOK : 2 * TOK, :] = others[d][m, q]

    left = jnp.concatenate([held[4 * i + s] for s in range(4)], axis=1)
    right = jnp.concatenate([p_own[...], p_other[...]], axis=0)
    out[...] = lax.dot_general(left, right, (((0,), (0,)), ((), ())), preferred_element_type=F32).astype(BF16)


def outer(tabs, mine, others, p_own, p_other):
    rows = pl.BlockSpec((4, 2, TOK, 128), lambda i, tab: (0, 0, 0, 0))
    return pl.pallas_call(
        outer_kernel,
        grid_spec=pltpu.PrefetchScalarGridSpec(
            num_scalar_prefetch=1,
            grid=(8,),
            in_specs=[rows] * 8 + [whole((TOK, COLS))] * 2,
            out_specs=pl.BlockSpec((512, COLS), lambda i, tab: (i, 0)),
            scratch_shapes=[pltpu.VMEM((32, 2 * TOK, 128), BF16)],
        ),
        out_shape=jax.ShapeDtypeStruct((4096, COLS), BF16),
        compiler_params=pltpu.CompilerParams(vmem_limit_bytes=VMEM, dimension_semantics=("arbitrary",)),
        cost_estimate=pl.CostEstimate(flops=4 * TOK * 4096 * COLS, bytes_accessed=12 << 20, transcendentals=0),
        name="head_outer",
    )(tabs, *mine, *others, p_own, p_other)


def total(parts):
    out = parts[0].astype(F32)
    for p in parts[1:]:
        out = out + p.astype(F32)
    return out.astype(BF16)


def shards(hidden, tangent_hidden, head, tangent_head, allowed):
    k, v = lax.axis_index("dp"), lax.axis_index("vocab")
    y, x = (v // 4) % 4, v % 4
    step = jnp.arange(16, dtype=jnp.int32)
    d, m = step // 4, step % 4
    by_x, by_y = m * 4 + (x - d + 4) % 4, ((y - d + 4) % 4) * 4 + m
    tab_own, tab_other = jnp.where(k == 0, by_x, by_y), jnp.where(k == 0, by_y, by_x)

    rows = jnp.concatenate([hidden, tangent_hidden], axis=0)
    column = spread(rows, depth_groups())
    plane = spread(column, middle_groups())
    mine = plane[:, :2]
    other = permute(plane[:, 2:], swap_pairs())
    others = [other] + [permute(other, shift(False, s)) for s in (1, 2, 3)]
    owns = [mine] + [permute(mine, shift(True, s)) for s in (1, 2, 3)]

    sent = scores(tab_other, others, head, tangent_head)
    got = permute(sent, swap_pairs())
    weights, tangent, stats = scores(tab_own, owns, head, tangent_head, got, allowed)
    every = lax.all_to_all(
        jnp.broadcast_to(stats[None], (64, 8, 128)), "vocab", split_axis=0, concat_axis=0, tiled=True
    )
    p_own = make_product(every, stats, weights, tangent)
    p_other = permute(p_own, swap_pairs())

    terms = back(tab_own, p_own, head)
    sums = total([terms[0]] + [permute(terms[s], shift(True, -s)) for s in (1, 2, 3)])
    terms = back(tab_other, p_other, head)
    sums_other = total([terms[0]] + [permute(terms[s], shift(False, -s)) for s in (1, 2, 3)])
    head_product = outer(jnp.concatenate([tab_own, tab_other]), owns, others, p_own, p_other)
    rest = permute(sums_other, swap_pairs())
    slab = jnp.concatenate([sums, rest], axis=1).reshape(16, TOK, 128)
    arrived = exchange(slab, plane_groups())
    hidden_product = jnp.sum(arrived.astype(F32), axis=0).astype(BF16)
    return head_product, hidden_product


def solution(mesh):
    place = P("dp", "vocab")
    return jax.shard_map(shards, mesh=mesh, in_specs=(place,) * 5, out_specs=(place, place), check_vma=False)
```

time: 782 us -> 184 us (0.24)
  blocking collectives: 372 us -> 45.9 us
  waiting for transfers between devices: 333 us -> 45.9 us
  Pallas kernels: 0 us -> 54 us
  matrix products: 34.1 us -> 0 us
  starting transfers between devices: 0.2 us -> 30.3 us
  local copies, waits for them, and re-layouts: 20.1 us -> 1.61 us
  between operations: 13.9 us -> 0.76 us
    reduce_scatter x3 -> x0, waiting for transfers between devices: 196 us -> none  [the longest x1 195 us: shards(): lax.psum_scatter(regrouped, 'vocab', scatter_dimension=1, tiled=True)]
    pmax x1 -> x0, blocking collectives: 148 us -> none  [shards(): top_logit = lax.pmax(local_top, 'vocab')]
    psum x1 -> x0, blocking collectives: 144 us -> none  [shards(): lax.psum((jnp.sum(weights, axis=1), jnp.sum(weights * tangent, axis=1)),...]
    all_gather x2 -> x0, waiting for transfers between devices: 136 us -> none  [the longest x1 76.6 us: shards(): lax.all_gather(hidden, 'vocab', axis=1, tiled=True)]
    all_gather x1 -> x0, blocking collectives: 57.8 us -> none  [shards(): product_all = lax.all_gather(product, 'dp', axis=0, tiled=True)]
    pallas_call x0 -> x6, Pallas kernels: none -> 54 us  [the longest x2 27 us: scores(): pl.pallas_call(functools.partial(score_kernel, own=own), grid_spec=pltpu....]
    ppermute x0 -> x16, waiting for transfers between devices: none -> 45.9 us  [permute(): return lax.ppermute(value, AXES, pairs)]
    dot_general x6 -> x0, matrix products: 34.1 us -> none  [the longest x1 9.46 us: contract_cols(): lax.dot_general(left, right, (((1,), (1,)), ((), ())), preferred_element_...]
  transfers between devices with their start and end apart: 5 -> 17, of which waited for: 3 -> 8; matrix products, arithmetic and copies ran while one was open for 6% -> 0% of each run, Pallas kernels for 0% -> 10%
where the time goes in v1:
time: 184 us; the launch traced here: 183 us
  Pallas kernels  54 us (29%)
  blocking collectives  45.9 us (25%)
  waiting for transfers between devices  45.9 us (25%)
  starting transfers between devices  30.3 us (16%)
  other arithmetic  4.23 us (2%)
    ppermute x16, waiting for transfers between devices, permute(): return lax.ppermute(value, AXES, pairs)  45.9 us
    all_to_all x2, blocking collectives, exchange(): lax.all_to_all(value, AXES, split_axis=0, concat_axis=0, tiled=True, axis...  28.4 us
    pallas_call x2, Pallas kernels, scores(): pl.pallas_call(functools.partial(score_kernel, own=own), grid_spec=pltpu....  27 us
    ppermute x16, starting transfers between devices, permute(): return lax.ppermute(value, AXES, pairs)  24.2 us
    all_to_all x1, blocking collectives, shards(): lax.all_to_all(jnp.broadcast_to(stats[None], (64, 8, 128)), 'vocab', spli...  17.5 us
    pallas_call x2, Pallas kernels, back(): pl.pallas_call(back_kernel, grid_spec=pltpu.PrefetchScalarGridSpec(num_sc...  16.7 us
    pallas_call x1, Pallas kernels, outer(): pl.pallas_call(outer_kernel, grid_spec=pltpu.PrefetchScalarGridSpec(num_s...  9.88 us
    all_to_all x1, starting transfers between devices, exchange(): lax.all_to_all(value, AXES, split_axis=0, concat_axis=0, tiled=True, axis...  6.05 us
  transfers between devices with their start and end apart: 17, of which 8 were waited for; matrix products, arithmetic and copies ran while one was open for 0% of the time, Pallas kernels for 10%

profile of v1, /device:TPU:1, one launch (start us, length us, event | category | flops | bytes accessed | tf_op | source)
XLA Modules:
  0.0 182.7 jit_solution(482120956050069589)
XLA Ops:
  0.6 0.8 pad_maximum_fusion.1
  1.5 0.1 broadcast_in_dim.6
  1.5 11.8 %all_to_all.20 = bf16[4,384,128]{2,1,0:T(8,128)(2,1)S(1)} all-to-all(bf16[4,384,128]{2,1,0:T(8,128)(2,1)S(1)} %broadcast_in_dim.6), channel_id=1, replica_groups={{0,16,32,48},{1,17,33,49},{2,18,34,50},{3,19,35,51},{4,20,36,52},{5,21,..., dimensions={0} | all-to-all | bytes 786432 | tf_op jit(solution)/shard_map/all_to_all | solution.py:62
  13.3 0.3 broadcast_in_dim.7
  13.6 16.7 %all_to_all.21 = bf16[4,4,384,128]{3,2,1,0:T(8,128)(2,1)S(1)} all-to-all(bf16[4,4,384,128]{3,2,1,0:T(8,128)(2,1)S(1)} %broadcast_in_dim.7), channel_id=1, replica_groups={{0,4,8,12},{1,5,9,13},{2,6,10,14},{3,7,11,15},{16,20,24,28},{17,21,25,2..., dimensions={0} | all-to-all | bytes 3145728 | tf_op jit(solution)/shard_map/all_to_all | solution.py:62
  30.2 0.1 fusion.5
  30.4 3.6 %collective-permute-start.3 = (bf16[4,2,384,128]{3,2,1,0:T(8,128)(2,1)S(1)}, bf16[4,2,384,128]{3,2,1,0:T(8,128)(2,1)S(1)}, u32[]{:S(2)}, u32[]{:S(2)}) collective-permute-start(bf16[4,2,384,128]{3,2,1,0:T(8,128)(2,1)S(1)} %get-tuple-element.24), channel_id=1, source_target_pairs={{0,64},{1,65},{2,66},{3,67},{4,68},{5,69},{6,70},{7,71},{8,72},{9,... | collective-permute-start | bytes 2359304 | tf_op jit(solution)/shard_map/ppermute | solution.py:58
  34.0 1.9 %collective-permute-done.3.refs_0_.refs_4_ = bf16[4,2,384,128]{3,2,1,0:T(8,128)(2,1)S(1)} collective-permute-done((bf16[4,2,384,128]{3,2,1,0:T(8,128)(2,1)S(1)}, bf16[4,2,384,128]{3,2,1,0:T(8,128)(2,1)S(1)}, u32[]{:S(2)}, u32[]{:S(2)}) %collective-permute-start.3) | collective-permute-done | bytes 786464 | tf_op jit(solution)/shard_map/ppermute | solution.py:58
  35.9 1.2 collective-permute-start.4
  37.1 2.5 %collective-permute-start.5 = (bf16[4,2,384,128]{3,2,1,0:T(8,128)(2,1)S(1)}, bf16[4,2,384,128]{3,2,1,0:T(8,128)(2,1)S(1)}, u32[]{:S(2)}, u32[]{:S(2)}) collective-permute-start(bf16[4,2,384,128]{3,2,1,0:T(8,128)(2,1)S(1)} %collective-permute-done.3.refs_0_.refs_4_), channel_id=1, source_target_pairs={{0,8},{1,9},{2,10},{3,11},{4,12},{5,13},{6,14},{7,15},{8,0},{9,1},... | collective-permute-start | bytes 2359304 | tf_op jit(solution)/shard_map/ppermute | solution.py:58
  39.6 1.2 collective-permute-start.6
  40.8 7.5 %collective-permute-done.4.refs_1_.refs_5_ = bf16[4,2,384,128]{3,2,1,0:T(8,128)(2,1)S(1)} collective-permute-done((bf16[4,2,384,128]{3,2,1,0:T(8,128)(2,1)S(1)}, bf16[4,2,384,128]{3,2,1,0:T(8,128)(2,1)S(1)}, u32[]{:S(2)}, u32[]{:S(2)}) %collective-permute-start.4) | collective-permute-done | bytes 786464 | tf_op jit(solution)/shard_map/ppermute | solution.py:58
  48.3 9.1 %collective-permute-done.5.refs_2_.refs_6_ = bf16[4,2,384,128]{3,2,1,0:T(8,128)(2,1)S(1)} collective-permute-done((bf16[4,2,384,128]{3,2,1,0:T(8,128)(2,1)S(1)}, bf16[4,2,384,128]{3,2,1,0:T(8,128)(2,1)S(1)}, u32[]{:S(2)}, u32[]{:S(2)}) %collective-permute-start.5) | collective-permute-done | bytes 786464 | tf_op jit(solution)/shard_map/ppermute | solution.py:58
  57.4 0.0 collective-permute-done.6.refs_3_.refs_7_
  57.4 12.9 %scores_other.1 = f32[384,1024]{1,0:T(8,128)} custom-call(s32[16]{0:T(128)S(1)} %broadcast_select_fusion.tab, bf16[4,2,384,128]{3,2,1,0:T(8,128)(2,1)S(1)} %collective-permute-done.3.refs_0_.refs_4_, bf16[4,2,384,128]{3,2,1,0:T(8,128)(2,1)S(1)} %collective-permute-done.4.refs_1_.refs_5_, bf16[4,2,384,128]{3,2,1,0:T(8,128)(2,1)S(1)} %collective-permute-done.5.refs_2_.refs_6_, ...), custom_call_target="tpu_custom_call" | custom-call | flops 4831838208 | bytes 20971520 | tf_op jit(solution)/shard_map/scores_other/pallas_call | solution.py:152
  70.3 1.6 collective-permute-start.7
  71.9 3.4 %collective-permute-start.1 = (bf16[4,2,384,128]{3,2,1,0:T(8,128)(2,1)S(1)}, bf16[4,2,384,128]{3,2,1,0:T(8,128)(2,1)}, u32[]{:S(2)}, u32[]{:S(2)}) collective-permute-start(bf16[4,2,384,128]{3,2,1,0:T(8,128)(2,1)S(1)} %get-tuple-element.25.refs_0_), channel_id=1, source_target_pairs={{0,2},{1,3},{2,0},{3,1},{4,6},{5,7},{6,4},{7,5},{8,10},{9,11},{10,... | collective-permute-start | bytes 2359304 | tf_op jit(solution)/shard_map/ppermute | solution.py:58
  75.3 0.1 copy.7.refs_13_
  75.5 8.8 %collective-permute-done.refs_1_ = bf16[4,2,384,128]{3,2,1,0:T(8,128)(2,1)S(1)} collective-permute-done((bf16[4,2,384,128]{3,2,1,0:T(8,128)(2,1)S(1)}, bf16[4,2,384,128]{3,2,1,0:T(8,128)(2,1)S(1)}, u32[]{:S(2)}, u32[]{:S(2)}) %collective-permute-start) | collective-permute-done | bytes 786464 | tf_op jit(solution)/shard_map/ppermute | solution.py:58
  84.2 9.3 %collective-permute-done.1.refs_2_ = bf16[4,2,384,128]{3,2,1,0:T(8,128)(2,1)} collective-permute-done((bf16[4,2,384,128]{3,2,1,0:T(8,128)(2,1)S(1)}, bf16[4,2,384,128]{3,2,1,0:T(8,128)(2,1)}, u32[]{:S(2)}, u32[]{:S(2)}) %collective-permute-start.1) | collective-permute-done | bytes 786464 | tf_op jit(solution)/shard_map/ppermute | solution.py:58
  93.5 0.0 collective-permute-done.2.refs_3_
  93.5 0.0 collective-permute-done.7.refs_12_
  93.5 14.2 %scores_own.1 = (f32[192,1024]{1,0:T(8,128)S(1)}, f32[192,1024]{1,0:T(8,128)S(1)}, f32[8,128]{1,0:T(8,128)S(1)}) custom-call(s32[16]{0:T(128)S(1)} %broadcast_select_fusion.1.tab, bf16[4,2,384,128]{3,2,1,0:T(8,128)(2,1)S(1)} %get-tuple-element.25.refs_0_, bf16[4,2,384,128]{3,2,1,0:T(8,128)(2,1)S(1)} %collective-permute-done.refs_1_, ...), custom_call_target="tpu_custom_call" | custom-call | flops 4831838208 | bytes 20971520 | tf_op jit(solution)/shard_map/scores_own/pallas_call | solution.py:152
  107.7 17.5 %all_to_all.22.every = f32[64,8,128]{2,1,0:T(8,128)S(1)} all-to-all(f32[64,8,128]{2,1,0:T(8,128)S(1)} %broadcast_in_dim.8), channel_id=1, replica_groups=mesh['dp'=2,'vocab'=64] {'vocab'}, dimensions={0} | all-to-all | bytes 524288 | tf_op jit(solution)/shard_map/all_to_all | solution.py:293
  125.2 0.4 product.1.refs_8_
  125.6 2.8 %collective-permute-start.8 = (bf16[192,1024]{1,0:T(8,128)(2,1)S(1)}, bf16[192,1024]{1,0:T(8,128)(2,1)S(1)}, u32[]{:S(2)}, u32[]{:S(2)}) collective-permute-start(bf16[192,1024]{1,0:T(8,128)(2,1)S(1)} %product.1.refs_8_), channel_id=1, source_target_pairs={{0,64},{1,65},{2,66},{3,67},{4,68},{5,69},{6,70},{7,71},{8,72},{9,... | collective-permute-start | bytes 1179656 | tf_op jit(solution)/shard_map/ppermute | solution.py:58
  128.5 1.3 collective-permute-done.8.refs_9_.product
  129.8 8.3 %hidden_back.3 = (bf16[4,2,192,128]{3,2,1,0:T(8,128)(2,1)S(1)}, bf16[4,2,192,128]{3,2,1,0:T(8,128)(2,1)S(1)}, bf16[4,2,192,128]{3,2,1,0:T(8,128)(2,1)S(1)}, bf16[4,2,192,128]{3,2,1,0:T(8,128)(2,1)S(1)}) custom-call(s32[16]{0:T(128)S(1)} %broadcast_select_fusion.tab, bf16[192,1024]{1,0:T(8,128)(2,1)S(1)} %collective-permute-done.8.refs_9_.product, ...), custom_call_target="tpu_custom_call" | custom-call | flops 1610612736 | bytes 10485760 | tf_op jit(solution)/shard_map/hidden_back/pallas_call | solution.py:217
  138.2 0.4 collective-permute-start.14
  138.5 1.5 collective-permute-start.13
  140.1 1.1 collective-permute-start.12
  141.2 8.3 %hidden_back.2 = (bf16[4,2,192,128]{3,2,1,0:T(8,128)(2,1)S(1)}, bf16[4,2,192,128]{3,2,1,0:T(8,128)(2,1)S(1)}, bf16[4,2,192,128]{3,2,1,0:T(8,128)(2,1)S(1)}, bf16[4,2,192,128]{3,2,1,0:T(8,128)(2,1)S(1)}) custom-call(s32[16]{0:T(128)S(1)} %broadcast_select_fusion.1.tab, bf16[192,1024]{1,0:T(8,128)(2,1)S(1)} %product.1.refs_8_, bf16[4096,1024]{1,0:T(8,128)(2,1)} %refs_3_.3, ...), custom_call_target="tpu_custom_call" | custom-call | flops 1610612736 | bytes 10485760 | tf_op jit(solution)/shard_map/hidden_back/pallas_call | solution.py:217
  149.6 0.2 collective-permute-start.11
  149.8 1.6 collective-permute-start.10
  151.3 0.0 collective-permute-done.14
  151.3 1.0 collective-permute-start.9
  152.3 0.0 collective-permute-done.13
  152.3 0.2 add_convert_fusion
  152.6 2.1 %collective-permute-start.15 = (bf16[4,2,192,128]{3,2,1,0:T(8,128)(2,1)S(1)}, bf16[4,2,192,128]{3,2,1,0:T(8,128)(2,1)S(1)}, u32[]{:S(2)}, u32[]{:S(2)}) collective-permute-start(bf16[4,2,192,128]{3,2,1,0:T(8,128)(2,1)S(1)} %add_convert_fusion), channel_id=1, source_target_pairs={{0,64},{1,65},{2,66},{3,67},{4,68},{5,69},{6,70},{7,71},{8,72},{9,... | collective-permute-start | bytes 1179656 | tf_op jit(solution)/shard_map/ppermute | solution.py:58
  154.7 7.3 %collective-permute-done.11 = bf16[4,2,192,128]{3,2,1,0:T(8,128)(2,1)S(1)} collective-permute-done((bf16[4,2,192,128]{3,2,1,0:T(8,128)(2,1)S(1)}, bf16[4,2,192,128]{3,2,1,0:T(8,128)(2,1)S(1)}, u32[]{:S(2)}, u32[]{:S(2)}) %collective-permute-start.11) | collective-permute-done | bytes 393248 | tf_op jit(solution)/shard_map/ppermute | solution.py:58
  162.0 0.6 collective-permute-done.9
  162.6 0.2 add_convert_fusion.1
  162.8 1.0 pad_maximum_fusion
  163.8 6.0 %all-to-all-start.3 = ((bf16[16,192,128]{2,1,0:T(8,128)(2,1)}), bf16[16,192,128]{2,1,0:T(8,128)(2,1)}, u32[]{:S(2)}, u32[]{:S(2)}) async-start(bf16[16,192,128]{2,1,0:T(8,128)(2,1)} %bitcast.1), calls=%async_computation.3 | async-start | bytes 1572864 | tf_op jit(solution)/shard_map/all_to_all | solution.py:62
  169.9 0.1 pad_add_fusion.tabs
  170.0 1.0 copy-done.2
  170.9 9.9 %head_outer.1 = bf16[4096,1024]{1,0:T(8,128)(2,1)} custom-call(s32[32]{0:T(128)S(1)} %pad_add_fusion.tabs, bf16[4,2,384,128]{3,2,1,0:T(8,128)(2,1)S(1)} %get-tuple-element.25.refs_0_, bf16[4,2,384,128]{3,2,1,0:T(8,128)(2,1)S(1)} %collective-permute-done.refs_1_, bf16[4,2,384,128]{3,2,1,0:T(8,128)(2,1)} %collective-permute-done.1.refs_2_, ...), custom_call_target="tpu_custom_call" | custom-call | flops 3221225472 | bytes 12582912 | tf_op jit(solution)/shard_map/head_outer/pallas_call | solution.py:251
  180.8 1.9 %reduce_sum.12 = bf16[192,128]{1,0:T(8,128)(2,1)} reduce(bf16[16,192,128]{2,1,0:T(8,128)(2,1)} %all-to-all-done.3, bf16[]{:T(256)} %constant.73.clone.1), dimensions={0}, to_apply=%region_0.1 | reduce | flops 368640 | bytes 835586 | tf_op jit(solution)/shard_map/reduce_sum | solution.py:307
  (16 shorter events, 0.1 us)
Async XLA Ops:
  30.4 5.5 %collective-permute-start.3 = (bf16[4,2,384,128]{3,2,1,0:T(8,128)(2,1)S(1)}, bf16[4,2,384,128]{3,2,1,0:T(8,128)(2,1)S(1)}, u32[]{:S(2)}, u32[]{:S(2)}) collective-permute-start(bf16[4,2,384,128]{3,2,1,0:T(8,128)(2,1)S(1)} %get-tuple-element.24), channel_id=1, source_target_pairs={{0,64},{1,65},{2,66},{3,67},{4,68},{5,69},{6,70},{7,71},{8,72},{9,... | collective-permute-start | bytes 2359304 | tf_op jit(solution)/shard_map/ppermute | solution.py:58
  35.9 12.3 %collective-permute-start.4 = (bf16[4,2,384,128]{3,2,1,0:T(8,128)(2,1)S(1)}, bf16[4,2,384,128]{3,2,1,0:T(8,128)(2,1)S(1)}, u32[]{:S(2)}, u32[]{:S(2)}) collective-permute-start(bf16[4,2,384,128]{3,2,1,0:T(8,128)(2,1)S(1)} %collective-permute-done.3.refs_0_.refs_4_), channel_id=1, source_target_pairs={{0,4},{1,5},{2,6},{3,7},{4,8},{5,9},{6,10},{7,11},{8,12},{9,13},{1... | collective-permute-start | bytes 2359304 | tf_op jit(solution)/shard_map/ppermute | solution.py:58
  37.1 20.3 %collective-permute-start.5 = (bf16[4,2,384,128]{3,2,1,0:T(8,128)(2,1)S(1)}, bf16[4,2,384,128]{3,2,1,0:T(8,128)(2,1)S(1)}, u32[]{:S(2)}, u32[]{:S(2)}) collective-permute-start(bf16[4,2,384,128]{3,2,1,0:T(8,128)(2,1)S(1)} %collective-permute-done.3.refs_0_.refs_4_), channel_id=1, source_target_pairs={{0,8},{1,9},{2,10},{3,11},{4,12},{5,13},{6,14},{7,15},{8,0},{9,1},... | collective-permute-start | bytes 2359304 | tf_op jit(solution)/shard_map/ppermute | solution.py:58
  39.6 17.8 %collective-permute-start.6 = (bf16[4,2,384,128]{3,2,1,0:T(8,128)(2,1)S(1)}, bf16[4,2,384,128]{3,2,1,0:T(8,128)(2,1)}, u32[]{:S(2)}, u32[]{:S(2)}) collective-permute-start(bf16[4,2,384,128]{3,2,1,0:T(8,128)(2,1)S(1)} %collective-permute-done.3.refs_0_.refs_4_), channel_id=1, source_target_pairs={{0,12},{1,13},{2,14},{3,15},{4,0},{5,1},{6,2},{7,3},{8,4},{9,5},{1... | collective-permute-start | bytes 2359304 | tf_op jit(solution)/shard_map/ppermute | solution.py:58
  40.7 34.6 %copy-start.3 = (s32[192,8]{0,1:T(8,128)S(1)}, s32[192,8]{0,1:T(8,128)}, u32[]{:S(2)}) copy-start(s32[192,8]{0,1:T(8,128)} %param.9) | copy-start | bytes 18436
  57.4 12.9 %copy-start = (bf16[4,2,384,128]{3,2,1,0:T(8,128)(2,1)}, bf16[4,2,384,128]{3,2,1,0:T(8,128)(2,1)S(1)}, u32[]{:S(2)}) copy-start(bf16[4,2,384,128]{3,2,1,0:T(8,128)(2,1)S(1)} %collective-permute-done.5.refs_2_.refs_6_) | copy-start | bytes 2359300
  70.3 23.2 %collective-permute-start.7 = (f32[384,1024]{1,0:T(8,128)}, f32[384,1024]{1,0:T(8,128)}, u32[]{:S(2)}, u32[]{:S(2)}) collective-permute-start(f32[384,1024]{1,0:T(8,128)} %scores_other.1), channel_id=1, source_target_pairs={{0,64},{1,65},{2,66},{3,67},{4,68},{5,69},{6,70},{7,71},{8,72},{9,... | collective-permute-start | bytes 4718600 | tf_op jit(solution)/shard_map/ppermute | solution.py:58
  71.9 12.3 %collective-permute-start = (bf16[4,2,384,128]{3,2,1,0:T(8,128)(2,1)S(1)}, bf16[4,2,384,128]{3,2,1,0:T(8,128)(2,1)S(1)}, u32[]{:S(2)}, u32[]{:S(2)}) collective-permute-start(bf16[4,2,384,128]{3,2,1,0:T(8,128)(2,1)S(1)} %get-tuple-element.25.refs_0_), channel_id=1, source_target_pairs={{0,1},{1,2},{2,3},{3,0},{4,5},{5,6},{6,7},{7,4},{8,9},{9,10},{10,1... | collective-permute-start | bytes 2359304 | tf_op jit(solution)/shard_map/ppermute | solution.py:58
  71.9 21.6 %collective-permute-start.1 = (bf16[4,2,384,128]{3,2,1,0:T(8,128)(2,1)S(1)}, bf16[4,2,384,128]{3,2,1,0:T(8,128)(2,1)}, u32[]{:S(2)}, u32[]{:S(2)}) collective-permute-start(bf16[4,2,384,128]{3,2,1,0:T(8,128)(2,1)S(1)} %get-tuple-element.25.refs_0_), channel_id=1, source_target_pairs={{0,2},{1,3},{2,0},{3,1},{4,6},{5,7},{6,4},{7,5},{8,10},{9,11},{10,... | collective-permute-start | bytes 2359304 | tf_op jit(solution)/shard_map/ppermute | solution.py:58
  75.3 18.2 %collective-permute-start.2 = (bf16[4,2,384,128]{3,2,1,0:T(8,128)(2,1)S(1)}, bf16[4,2,384,128]{3,2,1,0:T(8,128)(2,1)}, u32[]{:S(2)}, u32[]{:S(2)}) collective-permute-start(bf16[4,2,384,128]{3,2,1,0:T(8,128)(2,1)S(1)} %get-tuple-element.25.refs_0_), channel_id=1, source_target_pairs={{0,3},{1,0},{2,1},{3,2},{4,7},{5,4},{6,5},{7,6},{8,11},{9,8},{10,9... | collective-permute-start | bytes 2359304 | tf_op jit(solution)/shard_map/ppermute | solution.py:58
  125.6 4.2 %collective-permute-start.8 = (bf16[192,1024]{1,0:T(8,128)(2,1)S(1)}, bf16[192,1024]{1,0:T(8,128)(2,1)S(1)}, u32[]{:S(2)}, u32[]{:S(2)}) collective-permute-start(bf16[192,1024]{1,0:T(8,128)(2,1)S(1)} %product.1.refs_8_), channel_id=1, source_target_pairs={{0,64},{1,65},{2,66},{3,67},{4,68},{5,69},{6,70},{7,71},{8,72},{9,... | collective-permute-start | bytes 1179656 | tf_op jit(solution)/shard_map/ppermute | solution.py:58
  129.8 8.4 %copy-start.1 = (bf16[192,1024]{1,0:T(8,128)(2,1)}, bf16[192,1024]{1,0:T(8,128)(2,1)S(1)}, u32[]{:S(2)}) copy-start(bf16[192,1024]{1,0:T(8,128)(2,1)S(1)} %collective-permute-done.8.refs_9_.product) | copy-start | bytes 1179652
  138.2 13.2 %collective-permute-start.14 = (bf16[4,2,192,128]{3,2,1,0:T(8,128)(2,1)S(1)}, bf16[4,2,192,128]{3,2,1,0:T(8,128)(2,1)S(1)}, u32[]{:S(2)}, u32[]{:S(2)}) collective-permute-start(bf16[4,2,192,128]{3,2,1,0:T(8,128)(2,1)S(1)} %get-tuple-element.23), channel_id=1, source_target_pairs={{0,4},{1,5},{2,6},{3,7},{4,8},{5,9},{6,10},{7,11},{8,12},{9,13},{1... | collective-permute-start | bytes 1179656 | tf_op jit(solution)/shard_map/ppermute | solution.py:58
  138.5 13.8 %collective-permute-start.13 = (bf16[4,2,192,128]{3,2,1,0:T(8,128)(2,1)S(1)}, bf16[4,2,192,128]{3,2,1,0:T(8,128)(2,1)S(1)}, u32[]{:S(2)}, u32[]{:S(2)}) collective-permute-start(bf16[4,2,192,128]{3,2,1,0:T(8,128)(2,1)S(1)} %get-tuple-element.22), channel_id=1, source_target_pairs={{0,8},{1,9},{2,10},{3,11},{4,12},{5,13},{6,14},{7,15},{8,0},{9,1},... | collective-permute-start | bytes 1179656 | tf_op jit(solution)/shard_map/ppermute | solution.py:58
  140.1 12.3 %collective-permute-start.12 = (bf16[4,2,192,128]{3,2,1,0:T(8,128)(2,1)S(1)}, bf16[4,2,192,128]{3,2,1,0:T(8,128)(2,1)S(1)}, u32[]{:S(2)}, u32[]{:S(2)}) collective-permute-start(bf16[4,2,192,128]{3,2,1,0:T(8,128)(2,1)S(1)} %get-tuple-element.21), channel_id=1, source_target_pairs={{0,12},{1,13},{2,14},{3,15},{4,0},{5,1},{6,2},{7,3},{8,4},{9,5},{1... | collective-permute-start | bytes 1179656 | tf_op jit(solution)/shard_map/ppermute | solution.py:58
  149.6 12.4 %collective-permute-start.11 = (bf16[4,2,192,128]{3,2,1,0:T(8,128)(2,1)S(1)}, bf16[4,2,192,128]{3,2,1,0:T(8,128)(2,1)S(1)}, u32[]{:S(2)}, u32[]{:S(2)}) collective-permute-start(bf16[4,2,192,128]{3,2,1,0:T(8,128)(2,1)S(1)} %get-tuple-element.19), channel_id=1, source_target_pairs={{0,1},{1,2},{2,3},{3,0},{4,5},{5,6},{6,7},{7,4},{8,9},{9,10},{10,1... | collective-permute-start | bytes 1179656 | tf_op jit(solution)/shard_map/ppermute | solution.py:58
  149.8 12.2 %collective-permute-start.10 = (bf16[4,2,192,128]{3,2,1,0:T(8,128)(2,1)S(1)}, bf16[4,2,192,128]{3,2,1,0:T(8,128)(2,1)S(1)}, u32[]{:S(2)}, u32[]{:S(2)}) collective-permute-start(bf16[4,2,192,128]{3,2,1,0:T(8,128)(2,1)S(1)} %get-tuple-element.18), channel_id=1, source_target_pairs={{0,2},{1,3},{2,0},{3,1},{4,6},{5,7},{6,4},{7,5},{8,10},{9,11},{10,... | collective-permute-start | bytes 1179656 | tf_op jit(solution)/shard_map/ppermute | solution.py:58
  151.3 11.3 %collective-permute-start.9 = (bf16[4,2,192,128]{3,2,1,0:T(8,128)(2,1)S(1)}, bf16[4,2,192,128]{3,2,1,0:T(8,128)(2,1)S(1)}, u32[]{:S(2)}, u32[]{:S(2)}) collective-permute-start(bf16[4,2,192,128]{3,2,1,0:T(8,128)(2,1)S(1)} %get-tuple-element.17), channel_id=1, source_target_pairs={{0,3},{1,0},{2,1},{3,2},{4,7},{5,4},{6,5},{7,6},{8,11},{9,8},{10,9... | collective-permute-start | bytes 1179656 | tf_op jit(solution)/shard_map/ppermute | solution.py:58
  152.6 10.3 %collective-permute-start.15 = (bf16[4,2,192,128]{3,2,1,0:T(8,128)(2,1)S(1)}, bf16[4,2,192,128]{3,2,1,0:T(8,128)(2,1)S(1)}, u32[]{:S(2)}, u32[]{:S(2)}) collective-permute-start(bf16[4,2,192,128]{3,2,1,0:T(8,128)(2,1)S(1)} %add_convert_fusion), channel_id=1, source_target_pairs={{0,64},{1,65},{2,66},{3,67},{4,68},{5,69},{6,70},{7,71},{8,72},{9,... | collective-permute-start | bytes 1179656 | tf_op jit(solution)/shard_map/ppermute | solution.py:58
  163.8 17.0 %all-to-all-start.3 = ((bf16[16,192,128]{2,1,0:T(8,128)(2,1)}), bf16[16,192,128]{2,1,0:T(8,128)(2,1)}, u32[]{:S(2)}, u32[]{:S(2)}) async-start(bf16[16,192,128]{2,1,0:T(8,128)(2,1)} %bitcast.1), calls=%async_computation.3 | async-start | bytes 1572864 | tf_op jit(solution)/shard_map/all_to_all | solution.py:62
  170.0 1.0 copy-start.2
